TPU v7x, 128 devices: a whole 4x4x4 slice. The times are simulated.
128 devices in a mesh: row: 16 (over x, y_lo, core), col: 8 (over y_hi, z).
Axes of the slice: x: 4, y: 4 (y_hi: 2, y_lo: 2; y = y_hi * 2 + y_lo), z: 4, core: 2. Of those that a mesh axis runs over, the one named last changes fastest.
Arguments:
- blocks: bfloat16 [1024, 64, 128, 128], P('row', 'col'), may hold values from -0.109375 to 0.109375
- columns: int32 [1024, 64], P('row', 'col'), may hold values from 0 to 127
- counts: int32 [1024, 8], P('row', 'col'), may hold values from 1 to 8, as said below
- vectors: bfloat16 [1024, 32, 128], P(('col', 'row')), may hold values from -6 to 6
Outputs:
- first_image: bfloat16 [1024, 32, 128], P(('row', 'col'))
- first_back: bfloat16 [1024, 32, 128], P(('col', 'row'))
- second_image: bfloat16 [1024, 32, 128], P(('row', 'col'))
- second_back: bfloat16 [1024, 32, 128], P(('col', 'row'))
Inputs may be any that keep to these rules, and one draw needn't show every extreme that they name: `counts`: the live slots are the leading ones; the largest count, 8, is reached in every draw.
All inputs are finite; a program needn't handle non-finite values.
Results may differ from a plain program's by a relative error of at most 0.022.
Values may be sent and summed in bfloat16 or wider, within the bound.
A program may use at most 64 MiB of HBM per device.

v0:
```python
import jax
import jax.numpy as jnp
from jax import lax
from jax.sharding import PartitionSpec as P


def pick_blocks(column_vecs, columns, active):
    return column_vecs[columns] * active.astype(jnp.bfloat16)[:, :, None, None]


def forward_terms(blocks, picked):
    return jnp.einsum("isrc,iskc->ikr", blocks, picked, preferred_element_type=jnp.float32)


def adjoint_terms(blocks, columns, active, row_vecs, col_count):
    terms = jnp.einsum("isrc,ikr->iskc", blocks, row_vecs, preferred_element_type=jnp.float32)
    terms = terms * active.astype(jnp.float32)[:, :, None, None]
    slot_total = terms.shape[0] * terms.shape[1]
    return jax.ops.segment_sum(
        terms.reshape(slot_total, terms.shape[2], terms.shape[3]),
        columns.reshape(slot_total),
        num_segments=col_count,
    )


def body(blocks, columns, counts, vectors):
    vec_count = vectors.shape[0]
    col_count = vec_count * lax.axis_size("row")
    slot_ids = jnp.arange(columns.shape[1], dtype=jnp.int32)
    active = slot_ids[None, :] < counts
    results = []
    current = vectors
    for round_no in range(2):
        column_vecs = lax.all_gather(current, "row", axis=0, tiled=True)
        picked = pick_blocks(column_vecs, columns, active)
        forward_out = lax.psum_scatter(
            forward_terms(blocks, picked), "col", scatter_dimension=0, tiled=True
        ).astype(jnp.bfloat16)
        row_vecs = lax.all_gather(forward_out, "col", axis=0, tiled=True)
        partial_value = adjoint_terms(blocks, columns, active, row_vecs, col_count)
        adjoint_out = lax.psum_scatter(
            partial_value.astype(jnp.bfloat16), "row", scatter_dimension=0, tiled=True
        )
        results.append(forward_out)
        results.append(adjoint_out)
        current = adjoint_out
    return (results[0], results[1], results[2], results[3])


def solution(mesh):
    in_specs = (
        P("row", "col", None, None),
        P("row", "col"),
        P("row", "col"),
        P(("col", "row"), None, None),
    )
    out_specs = (
        P(("row", "col"), None, None),
        P(("col", "row"), None, None),
        P(("row", "col"), None, None),
        P(("col", "row"), None, None),
    )
    return jax.shard_map(body, mesh=mesh, in_specs=in_specs, out_specs=out_specs, check_vma=False)
```

profile of v0, /device:TPU:1, one launch (start us, length us, event | category | flops | bytes accessed | tf_op | source)
XLA Modules:
  0.0 563.6 jit_solution(17264336816287896016)
XLA Ops:
  7.2 0.7 all-gather.3.cloned.1.call-update
  7.9 0.7 compare_select_fusion
  8.6 0.1 copy.10
  8.7 0.1 reshape.62
  8.8 0.7 fusion.14
  9.6 36.2 %all-gather.3.cloned.1.call-done = bf16[128,32,128]{2,1,0:T(8,128)(2,1)} async-done(((bf16[8,32,128]{2,1,0:T(8,128)(2,1)}), bf16[128,32,128]{2,1,0:T(8,128)(2,1)}) %all-gather.3.cloned.1.call-update) | async-done | bytes 1048592 | tf_op jit(solution)/shard_map/all_gather | solution.py:34
  45.7 4.4 gather_fusion
  50.1 10.9 %fusion.6 = f32[64,32,128]{2,1,0:T(8,128)} fusion(bf16[64,8,128,128]{3,2,1,0:T(8,128)(2,1)} %param.4, bf16[64,8,32,128]{3,2,1,0:T(8,128)(2,1)} %bitcast.32, bf16[64,8]{1,0:T(8,128)(2,1)S(1)} %get-tuple-element.5), kind=kOutput, calls=%fused_computation.12 | convolution fusion | flops 538968064 | bytes 22021120 | tf_op jit(solution)/shard_map/isrc,iskc->ikr/dot_general | solution.py:12
  61.0 0.0 reduce-scatter.7.cloned.1.call-start
  61.1 0.1 copy.11
  61.2 0.1 reshape.78
  61.3 69.7 %reduce-scatter.5.cloned.1.call-done = f32[8,32,128]{2,1,0:T(8,128)} async-done(((f32[64,32,128]{2,1,0:T(8,128)}), f32[8,32,128]{2,1,0:T(8,128)}) %reduce-scatter.5.cloned.1.call-update) | async-done | bytes 131088 | tf_op jit(solution)/shard_map/reduce_scatter | solution.py:36
  130.9 0.9 convert_element_type.29
  131.9 29.4 %all_gather.13 = bf16[64,32,128]{2,1,0:T(8,128)(2,1)S(1)} all-gather(bf16[8,32,128]{2,1,0:T(8,128)(2,1)S(1)} %convert_element_type.29), channel_id=1, replica_groups=mesh['row'=16,'col'=8] {'col'}, dimensions={0}, use_global_device_ids=true | all-gather | bytes 589824 | tf_op jit(solution)/shard_map/all_gather | solution.py:39
  161.3 11.3 %broadcast_multiply_fusion.1 = f32[64,32,8,128]{3,1,2,0:T(8,128)} fusion(f32[64,8]{1,0:T(8,128)S(1)} %get-tuple-element.4, bf16[64,8,128,128]{3,2,1,0:T(8,128)(2,1)} %param.4, bf16[64,32,128]{2,1,0:T(8,128)(2,1)S(1)} %all_gather.13), kind=kOutput, calls=%fused_computation.7 | convolution fusion | flops 538968064 | bytes 25692160 | tf_op jit(solution)/shard_map/isrc,ikr->iskc/dot_general | solution.py:16
  172.7 0.2 broadcast.40.clone
  172.9 44.6 %scatter_fusion = f32[128,32,128]{2,1,0:T(8,128)S(1)} fusion(f32[128,32,128]{2,1,0:T(8,128)S(1)} %broadcast.40.clone, s32[512]{0:T(512)S(1)} %reshape.78, f32[512,32,128]{2,1,0:T(8,128)} %bitcast.30), kind=kCustom, calls=%fused_computation.2 | custom fusion | flops 2097152 | bytes 25167872 | tf_op jit(solution)/shard_map/scatter-add | solution.py:19
  217.5 1.2 convert_element_type.31
  218.7 0.0 all-gather.5.cloned.1.call-start
  218.7 64.0 %reduce-scatter.7.cloned.1.call-done = bf16[8,32,128]{2,1,0:T(8,128)(2,1)} async-done(((bf16[128,32,128]{2,1,0:T(8,128)(2,1)}), bf16[8,32,128]{2,1,0:T(8,128)(2,1)}) %reduce-scatter.7.cloned.1.call-update) | async-done | bytes 65552 | tf_op jit(solution)/shard_map/reduce_scatter | solution.py:41
  282.8 37.0 %all-gather.5.cloned.1.call-done = bf16[128,32,128]{2,1,0:T(8,128)(2,1)} async-done(((bf16[8,32,128]{2,1,0:T(8,128)(2,1)}), bf16[128,32,128]{2,1,0:T(8,128)(2,1)}) %all-gather.5.cloned.1.call-update) | async-done | bytes 1048592 | tf_op jit(solution)/shard_map/all_gather | solution.py:34
  319.8 4.4 gather_fusion.1
  324.1 10.9 %fusion.9 = f32[64,32,128]{2,1,0:T(8,128)} fusion(bf16[64,8,128,128]{3,2,1,0:T(8,128)(2,1)} %param.4, bf16[64,8,32,128]{3,2,1,0:T(8,128)(2,1)} %bitcast.31, bf16[64,8]{1,0:T(8,128)(2,1)S(1)} %get-tuple-element.5), kind=kOutput, calls=%fused_computation.13 | convolution fusion | flops 538968064 | bytes 22021120 | tf_op jit(solution)/shard_map/isrc,iskc->ikr/dot_general | solution.py:12
  335.1 0.0 reduce-scatter.11.cloned.1.call-start
  335.1 69.8 %reduce-scatter.9.cloned.1.call-done = f32[8,32,128]{2,1,0:T(8,128)} async-done(((f32[64,32,128]{2,1,0:T(8,128)}), f32[8,32,128]{2,1,0:T(8,128)}) %reduce-scatter.9.cloned.1.call-update) | async-done | bytes 131088 | tf_op jit(solution)/shard_map/reduce_scatter | solution.py:36
  405.0 0.9 convert_element_type.32
  405.9 29.6 %all_gather.15 = bf16[64,32,128]{2,1,0:T(8,128)(2,1)S(1)} all-gather(bf16[8,32,128]{2,1,0:T(8,128)(2,1)S(1)} %convert_element_type.32), channel_id=1, replica_groups=mesh['row'=16,'col'=8] {'col'}, dimensions={0}, use_global_device_ids=true | all-gather | bytes 589824 | tf_op jit(solution)/shard_map/all_gather | solution.py:39
  435.5 11.3 %broadcast_multiply_fusion = f32[64,32,8,128]{3,1,2,0:T(8,128)} fusion(f32[64,8]{1,0:T(8,128)S(1)} %get-tuple-element.4, bf16[64,8,128,128]{3,2,1,0:T(8,128)(2,1)} %param.4, bf16[64,32,128]{2,1,0:T(8,128)(2,1)S(1)} %all_gather.15), kind=kOutput, calls=%fused_computation.6 | convolution fusion | flops 538968064 | bytes 25692160 | tf_op jit(solution)/shard_map/isrc,ikr->iskc/dot_general | solution.py:16
  446.8 0.2 broadcast.40
  447.1 44.6 %scatter_fusion.1 = f32[128,32,128]{2,1,0:T(8,128)S(1)} fusion(f32[128,32,128]{2,1,0:T(8,128)S(1)} %broadcast.40, s32[512]{0:T(512)S(1)} %reshape.78, f32[512,32,128]{2,1,0:T(8,128)} %bitcast.29), kind=kCustom, calls=%fused_computation.3 | custom fusion | flops 2097152 | bytes 25167872 | tf_op jit(solution)/shard_map/scatter-add | solution.py:19
  491.6 1.2 convert_element_type.33
  492.9 63.9 %reduce-scatter.11.cloned.1.call-done = bf16[8,32,128]{2,1,0:T(8,128)(2,1)} async-done(((bf16[128,32,128]{2,1,0:T(8,128)(2,1)}), bf16[8,32,128]{2,1,0:T(8,128)(2,1)}) %reduce-scatter.11.cloned.1.call-update) | async-done | bytes 65552 | tf_op jit(solution)/shard_map/reduce_scatter | solution.py:41
  (15 shorter events, 0.2 us)
Async XLA Ops:
  7.2 38.6 %all-gather.3.cloned.1.call-start = ((), (), s32[]{:S(2)}) async-start(), calls=%async_computation.4 | async-start | bytes 1114112 | tf_op jit(solution)/shard_map/all_gather | solution.py:34
  7.9 123.0 %reduce-scatter.5.cloned.1.call-start = ((), (), s32[]{:S(2)}) async-start(), calls=%async_computation.5 | async-start | bytes 1179648 | tf_op jit(solution)/shard_map/reduce_scatter | solution.py:36
  50.1 11.0 %copy-start.2 = (s32[64,8]{0,1:T(8,128)S(1)}, s32[64,8]{0,1:T(8,128)}, u32[]{:S(2)}) copy-start(s32[64,8]{0,1:T(8,128)} %param.5) | copy-start | bytes 6148
  61.0 221.7 %reduce-scatter.7.cloned.1.call-start = ((), (), s32[]{:S(2)}) async-start(), calls=%async_computation.6 | async-start | bytes 1114112 | tf_op jit(solution)/shard_map/reduce_scatter | solution.py:41
  131.9 40.8 %copy-start = (bf16[8,32,128]{2,1,0:T(8,128)(2,1)}, bf16[8,32,128]{2,1,0:T(8,128)(2,1)S(1)}, u32[]{:S(2)}) copy-start(bf16[8,32,128]{2,1,0:T(8,128)(2,1)S(1)} %convert_element_type.29) | copy-start | bytes 196612
  218.7 101.1 %all-gather.5.cloned.1.call-start = ((), (), s32[]{:S(2)}) async-start(), calls=%async_computation.7 | async-start | bytes 1114112 | tf_op jit(solution)/shard_map/all_gather | solution.py:34
  282.7 122.2 %reduce-scatter.9.cloned.1.call-start = ((), (), s32[]{:S(2)}) async-start(), calls=%async_computation.8 | async-start | bytes 1179648 | tf_op jit(solution)/shard_map/reduce_scatter | solution.py:36
  335.1 221.7 %reduce-scatter.11.cloned.1.call-start = ((), (), s32[]{:S(2)}) async-start(), calls=%async_computation.9 | async-start | bytes 1114112 | tf_op jit(solution)/shard_map/reduce_scatter | solution.py:41
  405.9 40.9 %copy-start.1 = (bf16[8,32,128]{2,1,0:T(8,128)(2,1)}, bf16[8,32,128]{2,1,0:T(8,128)(2,1)S(1)}, u32[]{:S(2)}) copy-start(bf16[8,32,128]{2,1,0:T(8,128)(2,1)S(1)} %convert_element_type.32) | copy-start | bytes 196612
Sparse Core Ops, SparseCore 0:
  9.7 35.9 all-gather.2
  61.2 69.7 reduce-scatter.4
  218.8 63.8 reduce-scatter.6
  284.9 34.8 all-gather.4
  335.2 69.7 reduce-scatter.8
  493.0 63.7 reduce-scatter.10
where the time goes:
time: 569 us; the launch traced here: 564 us
  waiting for transfers between devices  341 us (60%)
  other arithmetic  94.7 us (17%)
  blocking collectives  59 us (10%)
  matrix products  44.5 us (8%)
  between operations  14.2 us (2%)
  local copies, waits for them, and re-layouts  9.62 us (2%)
    reduce_scatter x2, waiting for transfers between devices, body(): lax.psum_scatter(forward_terms(blocks, picked), 'col', scatter_dimension=...  139 us
    reduce_scatter x2, waiting for transfers between devices, body(): lax.psum_scatter(partial_value.astype(jnp.bfloat16), 'row', scatter_dimen...  128 us
    scatter-add x2, other arithmetic, adjoint_terms(): jax.ops.segment_sum(terms.reshape(slot_total, terms.shape[2], terms.shape...  89.1 us
    all_gather x2, waiting for transfers between devices, body(): column_vecs = lax.all_gather(current, 'row', axis=0, tiled=True)  73.2 us
    all_gather x2, blocking collectives, body(): row_vecs = lax.all_gather(forward_out, 'col', axis=0, tiled=True)  59 us
    dot_general x2, matrix products, adjoint_terms(): jnp.einsum('isrc,ikr->iskc', blocks, row_vecs, preferred_element_type=jnp...  22.7 us
    dot_general x2, matrix products, forward_terms(): jnp.einsum('isrc,iskc->ikr', blocks, picked, preferred_element_type=jnp.f...  21.8 us
  transfers between devices with their start and end apart: 6, of which 6 were waited for; matrix products, arithmetic and copies ran while one was open for 0% of the time, Pallas kernels for 0%

commit v1 on v0

v1 whole, which is shorter than its diff:
```python
import functools

import jax
import jax.numpy as jnp
from jax import lax
from jax.experimental import pallas as pl
from jax.experimental.pallas import tpu as pltpu
from jax.sharding import PartitionSpec as P

MESH = pl.DeviceIdType.MESH
NT = (((1,), (1,)), ((), ()))
F32 = jnp.float32
BF16 = jnp.bfloat16


def kernel(
    n_row, n_col, vb,
    blocks, gcol, perm, keep, last, vectors,
    out0, out1, out2, out3,
    w, cv, pb, rb, rv, tb, seg, sb, sib, hb, rr,
    load_sem, ag_send, ag_recv, fw_send, fw_recv, sc_send, sc_recv,
    gc_send, gc_recv, sx_send, sx_recv, sr_send, sr_recv,
):
    row = lax.axis_index("row")
    col = lax.axis_index("col")
    chips = n_row // 2
    chip = row // 2
    core = row % 2
    nnz = w.shape[0] // (n_col * vb)
    rows = n_col * vb
    slots = rows * nnz
    cols = n_row * vb
    k, bs = vectors.shape[1], vectors.shape[2]

    def peer(step):
        return (chip + step) % chips

    def cpeer(step):
        return (col + step) % n_col

    def load(d):
        part = pl.ds(d * vb * nnz, vb * nnz)
        return pltpu.make_async_copy(blocks.at[part], w.at[part], load_sem.at[d])

    for d in range(n_col):
        load(d).start()

    barrier = pltpu.get_barrier_semaphore()
    pl.semaphore_signal(barrier, inc=1, device_id={"row": chip * 2 + 1 - core}, device_id_type=MESH)

    def greet_chip(s, c):
        pl.semaphore_signal(barrier, inc=1, device_id={"row": peer(s) * 2 + core}, device_id_type=MESH)
        return c

    def greet_col(s, c):
        pl.semaphore_signal(barrier, inc=1, device_id={"col": cpeer(s)}, device_id_type=MESH)
        return c

    lax.fori_loop(1, chips, greet_chip, 0)
    lax.fori_loop(1, n_col, greet_col, 0)
    pl.semaphore_wait(barrier, 1 + (chips - 1) + (n_col - 1))

    zero = jnp.zeros((k, bs), F32)
    seg[slots] = zero

    sibling = {"row": chip * 2 + 1 - core}

    for rnd in range(2):
        src = vectors if rnd == 0 else out1
        image = out0 if rnd == 0 else out2
        back = out1 if rnd == 0 else out3
        cvr = cv.at[rnd]
        rbr = rb.at[rnd]
        rvr = rv.at[rnd]
        sibr = sib.at[rnd]
        rrr = rr.at[rnd]
        cvr[cols] = zero.astype(BF16)

        def shard(r):
            return cvr.at[pl.ds(r * vb, vb)]

        def gather(s):
            return pltpu.make_async_remote_copy(
                src_ref=src, dst_ref=shard(row), send_sem=ag_send.at[rnd, s], recv_sem=ag_recv.at[rnd, s],
                device_id={"row": peer(s) * 2 + core}, device_id_type=MESH)

        def gather_arrival(s):
            there = (chip + chips - s) % chips
            return pltpu.make_async_remote_copy(
                src_ref=src, dst_ref=shard(there * 2 + core), send_sem=ag_send.at[rnd, s], recv_sem=ag_recv.at[rnd, s],
                device_id={"row": peer(s) * 2 + core}, device_id_type=MESH)

        def forwarding(s):
            there = (chip + chips - s) % chips
            at = shard(there * 2 + core)
            return pltpu.make_async_remote_copy(
                src_ref=at, dst_ref=at, send_sem=fw_send.at[rnd, s], recv_sem=fw_recv.at[rnd, s],
                device_id=sibling, device_id_type=MESH)

        def forwarding_arrival(s):
            there = (chip + chips - s) % chips
            at = shard(there * 2 + 1 - core)
            return pltpu.make_async_remote_copy(
                src_ref=at, dst_ref=at, send_sem=fw_send.at[rnd, s], recv_sem=fw_recv.at[rnd, s],
                device_id=sibling, device_id_type=MESH)

        def own_out():
            return pltpu.make_async_remote_copy(
                src_ref=src, dst_ref=shard(row), send_sem=fw_send.at[rnd, 0], recv_sem=fw_recv.at[rnd, 0],
                device_id=sibling, device_id_type=MESH)

        def gather_start(s, c):
            gather(s).start()
            return c

        own_out().start()
        lax.fori_loop(1, chips, gather_start, 0)
        shard(row)[...] = src[...]

        def pass_on(s, c):
            gather_arrival(s).wait_recv()
            forwarding(s).start()
            return c

        lax.fori_loop(1, chips, pass_on, 0)
        pltpu.make_async_remote_copy(
            src_ref=src, dst_ref=shard(chip * 2 + 1 - core), send_sem=fw_send.at[rnd, 0], recv_sem=fw_recv.at[rnd, 0],
            device_id=sibling, device_id_type=MESH).wait_recv()

        def gather_end(s, c):
            forwarding_arrival(s).wait_recv()
            forwarding(s).wait_send()
            gather(s).wait_send()
            return c

        own_out().wait_send()
        lax.fori_loop(1, chips, gather_end, 0)

        if rnd == 0:
            for d in range(n_col):
                load(d).wait()

        def partial(d):
            def one(i, c):
                base = (d * vb + i) * nnz
                x = jnp.concatenate([cvr[gcol[base + q]] for q in range(nnz)], axis=1)
                m = jnp.concatenate([w[base + q] for q in range(nnz)], axis=1)
                pb[rnd, d, i] = lax.dot_general(x, m, NT, preferred_element_type=F32).astype(BF16)
                return c
            lax.fori_loop(0, vb, one, 0, unroll=4)

        def scatter(s):
            return pltpu.make_async_remote_copy(
                src_ref=pb.at[rnd, cpeer(s)], dst_ref=rbr.at[s], send_sem=sc_send.at[rnd, s], recv_sem=sc_recv.at[rnd, s],
                device_id={"col": cpeer(s)}, device_id_type=MESH)

        def forward_step(s, c):
            partial(cpeer(s))
            scatter(s).start()
            return c

        lax.fori_loop(1, n_col, forward_step, 0)
        partial(col)

        def scatter_end(s, c):
            scatter(s).wait()
            return c

        lax.fori_loop(1, n_col, scatter_end, 0)

        def reduce_rows(i, c):
            total = pb[rnd, col, i].astype(F32)
            for s in range(1, n_col):
                total += rbr[s, i].astype(F32)
            total = total.astype(BF16)
            image[i] = total
            rvr[col * vb + i] = total
            return c

        lax.fori_loop(0, vb, reduce_rows, 0)

        def rshard(d):
            return rvr.at[pl.ds(d * vb, vb)]

        def spread(s):
            return pltpu.make_async_remote_copy(
                src_ref=rshard(col), dst_ref=rshard(col), send_sem=gc_send.at[rnd, s], recv_sem=gc_recv.at[rnd, s],
                device_id={"col": cpeer(s)}, device_id_type=MESH)

        def spread_arrival(s):
            at = rshard((col + n_col - s) % n_col)
            return pltpu.make_async_remote_copy(
                src_ref=at, dst_ref=at, send_sem=gc_send.at[rnd, s], recv_sem=gc_recv.at[rnd, s],
                device_id={"col": cpeer(s)}, device_id_type=MESH)

        def spread_start(s, c):
            spread(s).start()
            return c

        lax.fori_loop(1, n_col, spread_start, 0)

        def terms(d):
            def one(i, c):
                at = d * vb + i
                v = rvr[at]
                for q in range(0, nnz, 2):
                    base = at * nnz + q
                    m = jnp.concatenate([w[base], w[base + 1]], axis=1)
                    r = jnp.dot(v, m, preferred_element_type=F32)
                    tb[base] = r[:, :bs]
                    tb[base + 1] = r[:, bs:]
                return c
            lax.fori_loop(0, vb, one, 0, unroll=4)

        terms(col)

        def terms_step(s, c):
            spread_arrival(s).wait_recv()
            terms((col + n_col - s) % n_col)
            return c

        lax.fori_loop(1, n_col, terms_step, 0)

        def spread_end(s, c):
            spread(s).wait_send()
            return c

        lax.fori_loop(1, n_col, spread_end, 0)

        def running(t, total):
            total = total * keep[t] + tb[perm[t]]
            seg[t] = total
            return total

        lax.fori_loop(0, slots, running, zero, unroll=8)

        def column_chunk(r):
            def one(i, c):
                sb[rnd, r, i] = seg[last[r * vb + i]].astype(BF16)
                return c
            lax.fori_loop(0, vb, one, 0, unroll=4)

        def swap(q):
            return pltpu.make_async_remote_copy(
                src_ref=sb.at[rnd, q * 2 + 1 - core], dst_ref=sibr.at[q], send_sem=sx_send.at[rnd, q], recv_sem=sx_recv.at[rnd, q],
                device_id=sibling, device_id_type=MESH)

        def swap_step(s, c):
            q = peer(s)
            column_chunk(q * 2 + 1 - core)
            swap(q).start()
            return c

        lax.fori_loop(1, chips + 1, swap_step, 0)

        def own_step(s, c):
            column_chunk(peer(s) * 2 + core)
            return c

        lax.fori_loop(1, chips + 1, own_step, 0)

        def scatter_row(s):
            return pltpu.make_async_remote_copy(
                src_ref=hb.at[rnd, s], dst_ref=rrr.at[s], send_sem=sr_send.at[rnd, s], recv_sem=sr_recv.at[rnd, s],
                device_id={"row": peer(s) * 2 + core}, device_id_type=MESH)

        def pair_step(s, c):
            q = peer(s)
            swap(q).wait()
            hb[rnd, s] = (sb[rnd, q * 2 + core].astype(F32) + sibr[q].astype(F32)).astype(BF16)
            scatter_row(s).start()
            return c

        lax.fori_loop(1, chips, pair_step, 0)
        swap(chip).wait()

        def scatter_row_end(s, c):
            scatter_row(s).wait()
            return c

        lax.fori_loop(1, chips, scatter_row_end, 0)

        def reduce_cols(i, c):
            total = sb[rnd, row, i].astype(F32) + sibr[chip, i].astype(F32)
            for s in range(1, chips):
                total += rrr[s, i].astype(F32)
            back[i] = total.astype(BF16)
            return c

        lax.fori_loop(0, vb, reduce_cols, 0)


def column_order(col, col_count):
    slots = col.shape[0]
    ids = jnp.arange(slots, dtype=jnp.int32)
    key = col * slots + ids
    rank = jnp.sum((key[None, :] < key[:, None]).astype(jnp.int32), axis=1)
    hit = (rank[:, None] == ids[None, :]).astype(jnp.int32)
    perm = jnp.sum(hit * ids[:, None], axis=0)
    ordered = jnp.sum(hit * col[:, None], axis=0)
    before = jnp.concatenate([jnp.full((1,), -1, jnp.int32), ordered[:-1]])
    keep = (ordered == before).astype(F32)
    js = jnp.arange(col_count, dtype=jnp.int32)
    upto = jnp.sum((col[None, :] <= js[:, None]).astype(jnp.int32), axis=1)
    some = jnp.sum((col[None, :] == js[:, None]).astype(jnp.int32), axis=1)
    last = jnp.where(some > 0, upto - 1, slots)
    return perm, keep, last


def body(n_row, n_col, blocks, columns, counts, vectors):
    rows, nnz, bs, _ = blocks.shape
    vb, k, _ = vectors.shape
    slots = rows * nnz
    cols = n_row * vb
    chips = n_row // 2
    active = jnp.arange(nnz, dtype=jnp.int32)[None, :] < counts
    gcol = jnp.where(active, columns, cols).astype(jnp.int32).reshape(slots)
    perm, keep, last = column_order(gcol, cols)
    any_space = pl.BlockSpec(memory_space=pl.ANY)
    smem = pl.BlockSpec(memory_space=pltpu.SMEM)
    vmem = pl.BlockSpec(memory_space=pltpu.VMEM)
    dma = pltpu.SemaphoreType.DMA
    outs = pl.pallas_call(
        functools.partial(kernel, n_row, n_col, vb),
        out_shape=[jax.ShapeDtypeStruct((vb, k, bs), BF16)] * 4,
        in_specs=[any_space, smem, smem, smem, smem, vmem],
        out_specs=[vmem] * 4,
        scratch_shapes=[
            pltpu.VMEM((slots, bs, bs), BF16),
            pltpu.VMEM((2, cols + 1, k, bs), BF16),
            pltpu.VMEM((2, n_col, vb, k, bs), BF16),
            pltpu.VMEM((2, n_col, vb, k, bs), BF16),
            pltpu.VMEM((2, rows, k, bs), BF16),
            pltpu.VMEM((slots, k, bs), F32),
            pltpu.VMEM((slots + 1, k, bs), F32),
            pltpu.VMEM((2, n_row, vb, k, bs), BF16),
            pltpu.VMEM((2, chips, vb, k, bs), BF16),
            pltpu.VMEM((2, chips, vb, k, bs), BF16),
            pltpu.VMEM((2, chips, vb, k, bs), BF16),
            dma((n_col,)),
            dma((2, chips)), dma((2, chips)),
            dma((2, chips)), dma((2, chips)),
            dma((2, n_col)), dma((2, n_col)),
            dma((2, n_col)), dma((2, n_col)),
            dma((2, chips)), dma((2, chips)),
            dma((2, chips)), dma((2, chips)),
        ],
        compiler_params=pltpu.CompilerParams(
            collective_id=0, has_side_effects=True, vmem_limit_bytes=56 << 20),
        name="krylov",
    )(blocks.reshape(slots, bs, bs), gcol, perm, keep, last, vectors)
    return tuple(outs)


def solution(mesh):
    in_specs = (
        P("row", "col", None, None),
        P("row", "col"),
        P("row", "col"),
        P(("col", "row"), None, None),
    )
    out_specs = (
        P(("row", "col"), None, None),
        P(("col", "row"), None, None),
        P(("row", "col"), None, None),
        P(("col", "row"), None, None),
    )
    run = functools.partial(body, mesh.shape["row"], mesh.shape["col"])
    return jax.shard_map(run, mesh=mesh, in_specs=in_specs, out_specs=out_specs, check_vma=False)
```

time: 569 us -> 111 us (0.20)
  waiting for transfers between devices: 341 us -> 0 us
  Pallas kernels: 0 us -> 101 us
  other arithmetic: 94.7 us -> 3.09 us
  blocking collectives: 59 us -> 0 us
  matrix products: 44.5 us -> 0 us
  between operations: 14.2 us -> 0.65 us
    reduce_scatter x4 -> x0, waiting for transfers between devices: 267 us -> none  [the longest x2 139 us: body(): lax.psum_scatter(forward_terms(blocks, picked), 'col', scatter_dimension=...]
    pallas_call x0 -> x1, Pallas kernels: none -> 101 us  [body(): pl.pallas_call(functools.partial(kernel, n_row, n_col, vb), out_shape=[ja...]
    scatter-add x2 -> x0, other arithmetic: 89.1 us -> none  [adjoint_terms(): jax.ops.segment_sum(terms.reshape(slot_total, terms.shape[2], terms.shape...]
    all_gather x2 -> x0, waiting for transfers between devices: 73.2 us -> none  [body(): column_vecs = lax.all_gather(current, 'row', axis=0, tiled=True)]
    all_gather x2 -> x0, blocking collectives: 59 us -> none  [body(): row_vecs = lax.all_gather(forward_out, 'col', axis=0, tiled=True)]
    dot_general x4 -> x0, matrix products: 44.5 us -> none  [the longest x2 22.7 us: adjoint_terms(): jnp.einsum('isrc,ikr->iskc', blocks, row_vecs, preferred_element_type=jnp...]
    gather x2 -> x0, local copies, waits for them, and re-layouts: 8.75 us -> none  [pick_blocks(): return column_vecs[columns] * active.astype(jnp.bfloat16)[:, :, None, None]]
    unnamed x7 -> x6, local copies, waits for them, and re-layouts: 0.1 us -> 5.89 us
  transfers between devices with their start and end apart: 6 -> 0, of which waited for: 6 -> 0; matrix products, arithmetic and copies ran while one was open for 0% -> 0% of each run, Pallas kernels for 0% -> 0%
where the time goes in v1:
time: 111 us
  Pallas kernels  101 us (91%)
  local copies, waits for them, and re-layouts  6.07 us (5%)
  other arithmetic  3.09 us (3%)
    pallas_call x1, Pallas kernels, body(): pl.pallas_call(functools.partial(kernel, n_row, n_col, vb), out_shape=[ja...  101 us
    unnamed x6, local copies, waits for them, and re-layouts  5.89 us

profile of v1, /device:TPU:1, one launch (start us, length us, event | category | flops | bytes accessed | tf_op | source)
XLA Modules:
  0.0 110.6 jit_solution(12082787468069818207)
XLA Ops:
  0.6 0.7 fusion
  1.3 0.1 copy.9
  1.4 0.1 reshape.36.gcol
  1.5 0.0 copy-start
  1.5 0.1 convert_reduce_fusion.1
  1.6 0.5 compare_select_fusion.last
  2.2 0.2 convert_reduce_fusion
  2.4 0.8 select_reduce_fusion
  3.3 0.7 fusion.1.keep
  3.9 0.0 copy-done
  3.9 100.8 %krylov.1 = (bf16[8,32,128]{2,1,0:T(8,128)(2,1)}, bf16[8,32,128]{2,1,0:T(8,128)(2,1)}, bf16[8,32,128]{2,1,0:T(8,128)(2,1)}, bf16[8,32,128]{2,1,0:T(8,128)(2,1)}) custom-call(bf16[512,128,128]{2,1,0:T(8,128)(2,1)} %bitcast.3, s32[512]{0:T(512)} %copy-done, s32[512]{0:T(512)} %get-tuple-element.7.perm, f32[512]{0:T(512)} %fusion.1.keep, ...), custom_call_target="tpu_custom_call" | custom-call | tf_op jit(solution)/shard_map/krylov/pallas_call | solution.py:323
  104.7 1.5 %copy.14 = bf16[8,32,128]{2,1,0:T(8,128)(2,1)} copy(bf16[8,32,128]{2,1,0:T(8,128)(2,1)} %get-tuple-element.12) | data formatting | bytes 131072
  106.2 1.5 %copy.15 = bf16[8,32,128]{2,1,0:T(8,128)(2,1)} copy(bf16[8,32,128]{2,1,0:T(8,128)(2,1)} %get-tuple-element.13) | data formatting | bytes 131072
  107.7 1.5 %copy.16 = bf16[8,32,128]{2,1,0:T(8,128)(2,1)} copy(bf16[8,32,128]{2,1,0:T(8,128)(2,1)} %get-tuple-element.14) | data formatting | bytes 131072
  109.2 1.5 %copy.17 = bf16[8,32,128]{2,1,0:T(8,128)(2,1)} copy(bf16[8,32,128]{2,1,0:T(8,128)(2,1)} %get-tuple-element.15) | data formatting | bytes 131072
  (1 shorter events, 0.0 us)
Async XLA Ops:
  1.5 2.4 %copy-start = (s32[512]{0:T(512)}, s32[512]{0:T(512)S(1)}, u32[]{:S(2)}) copy-start(s32[512]{0:T(512)S(1)} %reshape.36.gcol) | copy-start | bytes 6148

commit v2 on v0

v2 whole, which is shorter than its diff:
```python
import functools

import jax
import jax.numpy as jnp
from jax import lax
from jax.experimental import pallas as pl
from jax.experimental.pallas import tpu as pltpu
from jax.sharding import PartitionSpec as P

MESH = pl.DeviceIdType.MESH
F32 = jnp.float32
BF16 = jnp.bfloat16


def kernel(
    n_row, n_col, vb,
    blocks, gcol, perm, keep, last, vectors,
    out0, out1, out2, out3,
    w, wt, cv0, cv1, cv2, cv3, pb, rb, rv, tb, seg, sb, sib, hb, rr,
    load_sem, ag_send, ag_recv, fw_send, fw_recv, sc_send, sc_recv,
    gc_send, gc_recv, sx_send, sx_recv, sr_send, sr_recv,
):
    row = lax.axis_index("row")
    col = lax.axis_index("col")
    chips = n_row // 2
    nx, nz = chips // 2, n_col // 2
    chip, core = row // 2, row % 2
    x, y = chip // 2, chip % 2
    h, z = col // nz, col % nz
    rows = n_col * vb
    nnz = w.shape[0] // rows
    slots = rows * nnz
    cols = n_row * vb
    k2, bs = vectors.shape[1] // 2, vectors.shape[2]
    sibling = {"row": chip * 2 + 1 - core}

    def chip_to(e):
        return ((x + e % nx) % nx) * 2 + (y + e // nx) % 2

    def chip_from(e):
        return ((x + nx - e % nx) % nx) * 2 + (y + e // nx) % 2

    def col_to(e):
        return ((h + e // nz) % 2) * nz + (z + e % nz) % nz

    def col_from(e):
        return ((h + e // nz) % 2) * nz + (z + nz - e % nz) % nz

    def far_first(n, step):
        def one(s, c):
            step(n - 1 - s)
            return c
        lax.fori_loop(0, n - 1, one, 0)

    def load(d):
        part = pl.ds(d * vb * nnz, vb * nnz)
        return pltpu.make_async_copy(blocks.at[part], w.at[part], load_sem.at[d])

    for d in range(n_col):
        load(d).start()

    barrier = pltpu.get_barrier_semaphore()
    pl.semaphore_signal(barrier, inc=1, device_id=sibling, device_id_type=MESH)

    def greet_chip(e):
        pl.semaphore_signal(barrier, inc=1, device_id={"row": chip_to(e) * 2 + core}, device_id_type=MESH)

    def greet_col(e):
        pl.semaphore_signal(barrier, inc=1, device_id={"col": col_to(e)}, device_id_type=MESH)

    far_first(chips, greet_chip)
    far_first(n_col, greet_col)

    zero = jnp.zeros((k2, bs), F32)
    seg[slots] = zero

    class Part:
        def __init__(self, rnd, half):
            self.at = rnd * 2 + half
            self.mine = pl.ds(half * k2, k2)
            self.image = out0 if rnd == 0 else out2
            self.back = out1 if rnd == 0 else out3
            self.cv = (cv0, cv1, cv2, cv3)[self.at]
            self.pb, self.rb, self.rv = pb.at[self.at], rb.at[self.at], rv.at[self.at]
            self.sb, self.sib = sb.at[self.at], sib.at[self.at]
            self.hb, self.rr = hb.at[self.at], rr.at[self.at]

        def shard(self, r):
            return self.cv.at[pl.ds(r * vb, vb)]

        def copy(self, src, dst, send, recv, j, to):
            return pltpu.make_async_remote_copy(
                src_ref=src, dst_ref=dst, send_sem=send.at[self.at, j], recv_sem=recv.at[self.at, j],
                device_id=to, device_id_type=MESH)

        def gather(self, e, owner=None):
            at = self.shard(row if owner is None else owner)
            return self.copy(at, at, ag_send, ag_recv, e, {"row": chip_to(e) * 2 + core})

        def forwarding(self, e, owner):
            at = self.shard(owner)
            return self.copy(at, at, fw_send, fw_recv, e, sibling)

        def gather_start(self):
            self.cv[cols] = zero.astype(BF16)
            far_first(chips, lambda e: self.gather(e).start())
            self.forwarding(0, row).start()

        def pass_on(self):
            def one(s, c):
                e = s + 1
                owner = chip_from(e) * 2 + core
                self.gather(e, owner).wait_recv()
                self.forwarding(e, owner).start()
                return c
            lax.fori_loop(0, chips - 1, one, 0)

        def gather_end(self):
            def one(e, c):
                self.forwarding(e, chip_from(e) * 2 + 1 - core).wait_recv()
                return c
            lax.fori_loop(0, chips, one, 0)

        def partial(self, d):
            for i in range(vb):
                base = (d * vb + i) * nnz
                v = jnp.concatenate([self.cv[gcol[base + q]] for q in range(nnz)], axis=1)
                m = wt[pl.ds(base, nnz)].reshape(nnz * bs, bs)
                self.pb[d, i] = jnp.dot(v, m, preferred_element_type=F32).astype(BF16)

        def scatter(self, e):
            return self.copy(self.pb.at[col_to(e)], self.rb.at[e], sc_send, sc_recv, e, {"col": col_to(e)})

        def forward(self):
            def one(s, c):
                e = n_col - 1 - s
                self.partial(col_to(e))

                @pl.when(e > 0)
                def _():
                    self.scatter(e).start()
                return c
            lax.fori_loop(0, n_col, one, 0)

        def reduce_rows(self):
            far_first(n_col, lambda e: self.scatter(e).wait_recv())
            for i in range(vb):
                total = self.pb[col, i].astype(F32)
                for e in range(1, n_col):
                    total += self.rb[e, i].astype(F32)
                total = total.astype(BF16)
                self.image[i, self.mine] = total
                self.rv[col * vb + i] = total
            far_first(n_col, lambda e: self.spread(e).start())

        def spread(self, e, owner=None):
            at = self.rv.at[pl.ds((col if owner is None else owner) * vb, vb)]
            return self.copy(at, at, gc_send, gc_recv, e, {"col": col_to(e)})

        def terms(self, first, end):
            def one(e, c):
                d = col_from(e)

                @pl.when(e > 0)
                def _():
                    self.spread(e, d).wait_recv()
                for i in range(vb):
                    at = d * vb + i
                    v = self.rv[at]
                    for q in range(0, nnz, 2):
                        base = at * nnz + q
                        m = jnp.concatenate([w[base], w[base + 1]], axis=1)
                        r = jnp.dot(v, m, preferred_element_type=F32)
                        tb[base] = r[:, :bs]
                        tb[base + 1] = r[:, bs:]
                return c
            lax.fori_loop(first, end, one, 0)

        def column_chunk(self, r):
            for i in range(vb):
                self.sb[r, i] = seg[last[r * vb + i]].astype(BF16)

        def swap(self, q):
            return self.copy(self.sb.at[q * 2 + 1 - core], self.sib.at[q], sx_send, sx_recv, q, sibling)

        def combine(self):
            def running(t, total):
                total = total * keep[t] + tb[perm[t]]
                seg[t] = total
                return total

            lax.fori_loop(0, slots, running, zero, unroll=16)

            def theirs(s, c):
                q = chip_to(chips - 1 - s)
                self.column_chunk(q * 2 + 1 - core)
                self.swap(q).start()
                return c

            def ours(r, c):
                self.column_chunk(r * 2 + core)
                return c

            lax.fori_loop(0, chips, theirs, 0)
            lax.fori_loop(0, chips, ours, 0)

        def scatter_row(self, e):
            return self.copy(self.hb.at[e], self.rr.at[e], sr_send, sr_recv, e, {"row": chip_to(e) * 2 + core})

        def pair(self):
            def one(e):
                q = chip_to(e)
                self.swap(q).wait_recv()
                self.hb[e] = (self.sb[q * 2 + core].astype(F32) + self.sib[q].astype(F32)).astype(BF16)
                self.scatter_row(e).start()
            far_first(chips, one)
            self.swap(chip).wait_recv()

        def reduce_cols(self, following):
            far_first(chips, lambda e: self.scatter_row(e).wait_recv())
            for i in range(vb):
                total = self.sb[row, i].astype(F32) + self.sib[chip, i].astype(F32)
                for e in range(1, chips):
                    total += self.rr[e, i].astype(F32)
                total = total.astype(BF16)
                self.back[i, self.mine] = total
                if following is not None:
                    following.cv[row * vb + i] = total
            if following is not None:
                following.gather_start()

        def end(self):
            def by_chip(e):
                self.gather(e).wait_send()
                self.forwarding(e, row).wait_send()
                self.scatter_row(e).wait_send()
                self.swap(e).wait_send()

            def by_col(e):
                self.scatter(e).wait_send()
                self.spread(e).wait_send()

            far_first(chips, by_chip)
            far_first(n_col, by_col)
            self.forwarding(0, row).wait_send()
            self.swap(0).wait_send()

    parts = [[Part(rnd, half) for half in range(2)] for rnd in range(2)]
    a, b = parts[0]
    for part in (a, b):
        for i in range(vb):
            part.cv[row * vb + i] = vectors[i, part.mine]
    pl.semaphore_wait(barrier, 1 + (chips - 1) + (n_col - 1))
    a.gather_start()
    b.gather_start()

    def turn(d, c):
        load(d).wait()

        def one(i, cc):
            wt[d * vb * nnz + i] = w[d * vb * nnz + i].T
            return cc
        lax.fori_loop(0, vb * nnz, one, 0, unroll=8)
        return c

    early = n_col - n_col // 4
    lax.fori_loop(0, early, turn, 0)
    a.pass_on()
    lax.fori_loop(early, n_col, turn, 0)

    for rnd in range(2):
        a, b = parts[rnd]
        a.gather_end()
        a.forward()
        b.pass_on()
        b.gather_end()
        b.forward()
        a.reduce_rows()
        b.reduce_rows()
        a.terms(0, n_col)
        a.combine()
        b.terms(0, n_col // 2)
        a.pair()
        b.terms(n_col // 2, n_col)
        b.combine()
        b.pair()
        following = parts[1] if rnd == 0 else (None, None)
        a.reduce_cols(following[0])
        b.reduce_cols(following[1])
        if rnd == 0:
            following[0].pass_on()

    for pair in parts:
        for part in pair:
            part.end()


def copy_out(*refs):
    n = len(refs) // 2
    for j in range(n):
        refs[n + j][...] = refs[j][...]


def column_order(col, col_count):
    slots = col.shape[0]
    ids = jnp.arange(slots, dtype=jnp.int32)
    key = col * slots + ids
    rank = jnp.sum((key[None, :] < key[:, None]).astype(jnp.int32), axis=1)
    hit = (rank[:, None] == ids[None, :]).astype(jnp.int32)
    perm = jnp.sum(hit * ids[:, None], axis=0)
    ordered = jnp.sum(hit * col[:, None], axis=0)
    before = jnp.concatenate([jnp.full((1,), -1, jnp.int32), ordered[:-1]])
    keep = (ordered == before).astype(F32)
    js = jnp.arange(col_count, dtype=jnp.int32)
    upto = jnp.sum((col[None, :] <= js[:, None]).astype(jnp.int32), axis=1)
    some = jnp.sum((col[None, :] == js[:, None]).astype(jnp.int32), axis=1)
    last = jnp.where(some > 0, upto - 1, slots)
    return perm, keep, last


def body(n_row, n_col, blocks, columns, counts, vectors):
    rows, nnz, bs, _ = blocks.shape
    vb, k, _ = vectors.shape
    k2 = k // 2
    slots = rows * nnz
    cols = n_row * vb
    chips = n_row // 2
    active = jnp.arange(nnz, dtype=jnp.int32)[None, :] < counts
    gcol = jnp.where(active, columns, cols).astype(jnp.int32).reshape(slots)
    perm, keep, last = column_order(gcol, cols)
    any_space = pl.BlockSpec(memory_space=pl.ANY)
    smem = pl.BlockSpec(memory_space=pltpu.SMEM)
    vmem = pl.BlockSpec(memory_space=pltpu.VMEM)
    dma = pltpu.SemaphoreType.DMA
    result = [jax.ShapeDtypeStruct((vb, k, bs), BF16)] * 4
    outs = pl.pallas_call(
        functools.partial(kernel, n_row, n_col, vb),
        out_shape=result,
        in_specs=[any_space, smem, smem, smem, smem, vmem],
        out_specs=[vmem] * 4,
        scratch_shapes=[
            pltpu.VMEM((slots, bs, bs), BF16),
            pltpu.VMEM((slots, bs, bs), BF16),
            *[pltpu.VMEM((cols + 1, k2, bs), BF16)] * 4,
            pltpu.VMEM((4, n_col, vb, k2, bs), BF16),
            pltpu.VMEM((4, n_col, vb, k2, bs), BF16),
            pltpu.VMEM((4, rows, k2, bs), BF16),
            pltpu.VMEM((slots, k2, bs), F32),
            pltpu.VMEM((slots + 1, k2, bs), F32),
            pltpu.VMEM((4, n_row, vb, k2, bs), BF16),
            pltpu.VMEM((4, chips, vb, k2, bs), BF16),
            pltpu.VMEM((4, chips, vb, k2, bs), BF16),
            pltpu.VMEM((4, chips, vb, k2, bs), BF16),
            dma((n_col,)),
            dma((4, chips)), dma((4, chips)),
            dma((4, chips)), dma((4, chips)),
            dma((4, n_col)), dma((4, n_col)),
            dma((4, n_col)), dma((4, n_col)),
            dma((4, chips)), dma((4, chips)),
            dma((4, chips)), dma((4, chips)),
        ],
        compiler_params=pltpu.CompilerParams(
            collective_id=0, has_side_effects=True, vmem_limit_bytes=58 << 20),
        name="krylov",
    )(blocks.reshape(slots, bs, bs), gcol, perm, keep, last, vectors)
    outs = pl.pallas_call(
        copy_out,
        out_shape=result,
        in_specs=[vmem] * 4,
        out_specs=[vmem] * 4,
        name="results",
    )(*outs)
    return tuple(outs)


def solution(mesh):
    in_specs = (
        P("row", "col", None, None),
        P("row", "col"),
        P("row", "col"),
        P(("col", "row"), None, None),
    )
    out_specs = (
        P(("row", "col"), None, None),
        P(("col", "row"), None, None),
        P(("row", "col"), None, None),
        P(("col", "row"), None, None),
    )
    run = functools.partial(body, mesh.shape["row"], mesh.shape["col"])
    return jax.shard_map(run, mesh=mesh, in_specs=in_specs, out_specs=out_specs, check_vma=False)
```

time: 569 us -> 92.8 us (0.16)
  waiting for transfers between devices: 341 us -> 0 us
  other arithmetic: 94.7 us -> 3.09 us
  Pallas kernels: 0 us -> 88.7 us
  blocking collectives: 59 us -> 0 us
  matrix products: 44.5 us -> 0 us
  between operations: 14.2 us -> 0.65 us
  local copies, waits for them, and re-layouts: 9.62 us -> 0.18 us
    reduce_scatter x4 -> x0, waiting for transfers between devices: 267 us -> none  [the longest x2 139 us: body(): lax.psum_scatter(forward_terms(blocks, picked), 'col', scatter_dimension=...]
    scatter-add x2 -> x0, other arithmetic: 89.1 us -> none  [adjoint_terms(): jax.ops.segment_sum(terms.reshape(slot_total, terms.shape[2], terms.shape...]
    pallas_call x0 -> x2, Pallas kernels: none -> 88.7 us  [the longest x1 87 us: body(): pl.pallas_call(functools.partial(kernel, n_row, n_col, vb), out_shape=res...]
    all_gather x2 -> x0, waiting for transfers between devices: 73.2 us -> none  [body(): column_vecs = lax.all_gather(current, 'row', axis=0, tiled=True)]
    all_gather x2 -> x0, blocking collectives: 59 us -> none  [body(): row_vecs = lax.all_gather(forward_out, 'col', axis=0, tiled=True)]
    dot_general x4 -> x0, matrix products: 44.5 us -> none  [the longest x2 22.7 us: adjoint_terms(): jnp.einsum('isrc,ikr->iskc', blocks, row_vecs, preferred_element_type=jnp...]
    gather x2 -> x0, local copies, waits for them, and re-layouts: 8.75 us -> none  [pick_blocks(): return column_vecs[columns] * active.astype(jnp.bfloat16)[:, :, None, None]]
  transfers between devices with their start and end apart: 6 -> 0, of which waited for: 6 -> 0; matrix products, arithmetic and copies ran while one was open for 0% -> 0% of each run, Pallas kernels for 0% -> 0%
where the time goes in v2:
time: 92.8 us; the launch traced here: 92.6 us
  Pallas kernels  88.7 us (96%)
  other arithmetic  3.09 us (3%)
    pallas_call x1, Pallas kernels, body(): pl.pallas_call(functools.partial(kernel, n_row, n_col, vb), out_shape=res...  87 us

profile of v2, /device:TPU:1, one launch (start us, length us, event | category | flops | bytes accessed | tf_op | source)
XLA Modules:
  0.0 92.6 jit_solution(7500521670052132021)
XLA Ops:
  0.6 0.7 fusion
  1.3 0.1 copy.9
  1.4 0.1 reshape.36.gcol
  1.5 0.0 copy-start
  1.5 0.1 convert_reduce_fusion.1
  1.6 0.5 compare_select_fusion.last
  2.2 0.2 convert_reduce_fusion
  2.4 0.8 select_reduce_fusion
  3.3 0.7 fusion.1.keep
  3.9 0.0 copy-done
  3.9 87.0 %krylov.1 = (bf16[8,32,128]{2,1,0:T(8,128)(2,1)}, bf16[8,32,128]{2,1,0:T(8,128)(2,1)}, bf16[8,32,128]{2,1,0:T(8,128)(2,1)}, bf16[8,32,128]{2,1,0:T(8,128)(2,1)}) custom-call(bf16[512,128,128]{2,1,0:T(8,128)(2,1)} %bitcast.3, s32[512]{0:T(512)} %copy-done, s32[512]{0:T(512)} %get-tuple-element.15.perm, f32[512]{0:T(512)} %fusion.1.keep, ...), custom_call_target="tpu_custom_call" | custom-call | tf_op jit(solution)/shard_map/krylov/pallas_call | solution.py:336
  90.9 1.6 %results.1 = (bf16[8,32,128]{2,1,0:T(8,128)(2,1)}, bf16[8,32,128]{2,1,0:T(8,128)(2,1)}, bf16[8,32,128]{2,1,0:T(8,128)(2,1)}, bf16[8,32,128]{2,1,0:T(8,128)(2,1)}) custom-call(bf16[8,32,128]{2,1,0:T(8,128)(2,1)} %get-tuple-element.8.refs_0_, bf16[8,32,128]{2,1,0:T(8,128)(2,1)} %get-tuple-element.9.refs_1_, bf16[8,32,128]{2,1,0:T(8,128)(2,1)} %get-tuple-element.10.refs_2_, ...), custom_call_target="tpu_custom_call" | custom-call | tf_op jit(solution)/shard_map/results/pallas_call | solution.py:366
  (1 shorter events, 0.0 us)
Async XLA Ops:
  1.5 2.4 %copy-start = (s32[512]{0:T(512)}, s32[512]{0:T(512)S(1)}, u32[]{:S(2)}) copy-start(s32[512]{0:T(512)S(1)} %reshape.36.gcol) | copy-start | bytes 6148

commit v3 on v2

--- a/solution.py
+++ b/solution.py
@@ -14,10 +14,11 @@
 
 def kernel(
     n_row, n_col, vb,
-    blocks, gcol, perm, keep, last, vectors,
+    blocks, columns, vectors,
     out0, out1, out2, out3,
-    w, wt, cv0, cv1, cv2, cv3, pb, rb, rv, tb, seg, sb, sib, hb, rr,
-    load_sem, ag_send, ag_recv, fw_send, fw_recv, sc_send, sc_recv,
+    perm_v, keep_v, last_v, perm, keep, last, gcol,
+    w, wt, cv0, cv1, cv2, cv3, pb, rb, rv, tb0, tb1, seg, sb, sib, hb, rr,
+    load_sem, order_sem, ag_send, ag_recv, fw_send, fw_recv, sc_send, sc_recv,
     gc_send, gc_recv, sx_send, sx_recv, sr_send, sr_recv,
 ):
     row = lax.axis_index("row")
@@ -46,11 +47,19 @@
     def col_from(e):
         return ((h + e // nz) % 2) * nz + (z + nz - e % nz) % nz
 
-    def far_first(n, step):
-        def one(s, c):
-            step(n - 1 - s)
-            return c
-        lax.fori_loop(0, n - 1, one, 0)
+    def hops(e, ring, across):
+        return min(e % ring, ring - e % ring) + across * (e // ring)
+
+    far_chips = sorted(range(1, chips), key=lambda e: -hops(e, nx, 1))
+    far_cols = sorted(range(1, n_col), key=lambda e: -hops(e, nz, 2))
+
+    def each_chip(step):
+        for e in far_chips:
+            step(e)
+
+    def each_col(step):
+        for e in far_cols:
+            step(e)
 
     def load(d):
         part = pl.ds(d * vb * nnz, vb * nnz)
@@ -68,11 +77,11 @@
     def greet_col(e):
         pl.semaphore_signal(barrier, inc=1, device_id={"col": col_to(e)}, device_id_type=MESH)
 
-    far_first(chips, greet_chip)
-    far_first(n_col, greet_col)
+    each_chip(greet_chip)
+    each_col(greet_col)
 
     zero = jnp.zeros((k2, bs), F32)
-    seg[slots] = zero
+    seg[slots] = zero.astype(BF16)
 
     class Part:
         def __init__(self, rnd, half):
@@ -81,6 +90,7 @@
             self.image = out0 if rnd == 0 else out2
             self.back = out1 if rnd == 0 else out3
             self.cv = (cv0, cv1, cv2, cv3)[self.at]
+            self.tb = (tb0, tb1)[half]
             self.pb, self.rb, self.rv = pb.at[self.at], rb.at[self.at], rv.at[self.at]
             self.sb, self.sib = sb.at[self.at], sib.at[self.at]
             self.hb, self.rr = hb.at[self.at], rr.at[self.at]
@@ -103,17 +113,16 @@
 
         def gather_start(self):
             self.cv[cols] = zero.astype(BF16)
-            far_first(chips, lambda e: self.gather(e).start())
+            each_chip(lambda e: self.gather(e).start())
             self.forwarding(0, row).start()
 
-        def pass_on(self):
-            def one(s, c):
-                e = s + 1
+        def pass_on(self, first, end):
+            def one(e, c):
                 owner = chip_from(e) * 2 + core
                 self.gather(e, owner).wait_recv()
                 self.forwarding(e, owner).start()
                 return c
-            lax.fori_loop(0, chips - 1, one, 0)
+            lax.fori_loop(first, end, one, 0)
 
         def gather_end(self):
             def one(e, c):
@@ -122,16 +131,19 @@
             lax.fori_loop(0, chips, one, 0)
 
         def partial(self, d):
+            done = []
             for i in range(vb):
                 base = (d * vb + i) * nnz
-                v = jnp.concatenate([self.cv[gcol[base + q]] for q in range(nnz)], axis=1)
+                v = jnp.concatenate([self.cv[gcol[0, base + q]] for q in range(nnz)], axis=1)
                 m = wt[pl.ds(base, nnz)].reshape(nnz * bs, bs)
-                self.pb[d, i] = jnp.dot(v, m, preferred_element_type=F32).astype(BF16)
+                done.append(jnp.dot(v, m, preferred_element_type=F32).astype(BF16))
+            for i in range(vb):
+                self.pb[d, i] = done[i]
 
         def scatter(self, e):
             return self.copy(self.pb.at[col_to(e)], self.rb.at[e], sc_send, sc_recv, e, {"col": col_to(e)})
 
-        def forward(self):
+        def forward(self, first, end):
             def one(s, c):
                 e = n_col - 1 - s
                 self.partial(col_to(e))
@@ -140,18 +152,17 @@
                 def _():
                     self.scatter(e).start()
                 return c
-            lax.fori_loop(0, n_col, one, 0)
+            lax.fori_loop(first, end, one, 0)
 
         def reduce_rows(self):
-            far_first(n_col, lambda e: self.scatter(e).wait_recv())
-            for i in range(vb):
-                total = self.pb[col, i].astype(F32)
-                for e in range(1, n_col):
-                    total += self.rb[e, i].astype(F32)
-                total = total.astype(BF16)
-                self.image[i, self.mine] = total
-                self.rv[col * vb + i] = total
-            far_first(n_col, lambda e: self.spread(e).start())
+            each_col(lambda e: self.scatter(e).wait_recv())
+            total = self.pb[col].astype(F32)
+            for e in range(1, n_col):
+                total += self.rb[e].astype(F32)
+            total = total.astype(BF16)
+            self.rv[pl.ds(col * vb, vb)] = total
+            each_col(lambda e: self.spread(e).start())
+            self.image[:, self.mine] = total
 
         def spread(self, e, owner=None):
             at = self.rv.at[pl.ds((col if owner is None else owner) * vb, vb)]
@@ -167,29 +178,42 @@
                 for i in range(vb):
                     at = d * vb + i
                     v = self.rv[at]
+                    done = []
                     for q in range(0, nnz, 2):
                         base = at * nnz + q
                         m = jnp.concatenate([w[base], w[base + 1]], axis=1)
                         r = jnp.dot(v, m, preferred_element_type=F32)
-                        tb[base] = r[:, :bs]
-                        tb[base + 1] = r[:, bs:]
+                        done += [r[:, :bs], r[:, bs:]]
+                    for q in range(nnz):
+                        self.tb[at * nnz + q] = done[q]
                 return c
             lax.fori_loop(first, end, one, 0)
 
         def column_chunk(self, r):
+            ends = [seg[last[0, r * vb + i]] for i in range(vb)]
             for i in range(vb):
-                self.sb[r, i] = seg[last[r * vb + i]].astype(BF16)
+                self.sb[r, i] = ends[i]
 
         def swap(self, q):
             return self.copy(self.sb.at[q * 2 + 1 - core], self.sib.at[q], sx_send, sx_recv, q, sibling)
 
         def combine(self):
-            def running(t, total):
-                total = total * keep[t] + tb[perm[t]]
-                seg[t] = total
+            def running(u, total):
+                read = [self.tb[perm[0, u * 16 + q]] for q in range(16)]
+                sums = []
+                for first in range(0, 16, 4):
+                    chain, value = None, None
+                    for q in range(first, first + 4):
+                        stay = keep[0, u * 16 + q]
+                        chain = stay if q == first else chain * stay
+                        value = read[q] if q == first else value * stay + read[q]
+                        sums.append(total * chain + value)
+                    total = sums[-1]
+                for q in range(16):
+                    seg[u * 16 + q] = sums[q].astype(BF16)
                 return total
 
-            lax.fori_loop(0, slots, running, zero, unroll=16)
+            lax.fori_loop(0, slots // 16, running, zero)
 
             def theirs(s, c):
                 q = chip_to(chips - 1 - s)
@@ -213,21 +237,19 @@
                 self.swap(q).wait_recv()
                 self.hb[e] = (self.sb[q * 2 + core].astype(F32) + self.sib[q].astype(F32)).astype(BF16)
                 self.scatter_row(e).start()
-            far_first(chips, one)
+            each_chip(one)
             self.swap(chip).wait_recv()
 
         def reduce_cols(self, following):
-            far_first(chips, lambda e: self.scatter_row(e).wait_recv())
-            for i in range(vb):
-                total = self.sb[row, i].astype(F32) + self.sib[chip, i].astype(F32)
-                for e in range(1, chips):
-                    total += self.rr[e, i].astype(F32)
-                total = total.astype(BF16)
-                self.back[i, self.mine] = total
-                if following is not None:
-                    following.cv[row * vb + i] = total
+            each_chip(lambda e: self.scatter_row(e).wait_recv())
+            total = self.sb[row].astype(F32) + self.sib[chip].astype(F32)
+            for e in range(1, chips):
+                total += self.rr[e].astype(F32)
+            total = total.astype(BF16)
             if following is not None:
+                following.cv[pl.ds(row * vb, vb)] = total
                 following.gather_start()
+            self.back[:, self.mine] = total
 
         def end(self):
             def by_chip(e):
@@ -240,8 +262,8 @@
                 self.scatter(e).wait_send()
                 self.spread(e).wait_send()
 
-            far_first(chips, by_chip)
-            far_first(n_col, by_col)
+            each_chip(by_chip)
+            each_col(by_col)
             self.forwarding(0, row).wait_send()
             self.swap(0).wait_send()
 
@@ -263,36 +285,55 @@
         lax.fori_loop(0, vb * nnz, one, 0, unroll=8)
         return c
 
+    column_order(columns, nnz, cols, perm_v, keep_v, last_v)
+    moves = [
+        pltpu.make_async_copy(src, dst, order_sem.at[j])
+        for j, (src, dst) in enumerate(((perm_v, perm), (keep_v, keep), (last_v, last), (columns, gcol)))
+    ]
+    for move in moves:
+        move.start()
+    for move in moves:
+        move.wait()
+
     early = n_col - n_col // 4
     lax.fori_loop(0, early, turn, 0)
-    a.pass_on()
+    a.pass_on(1, chips)
     lax.fori_loop(early, n_col, turn, 0)
 
+    near, half = (chips + 1) // 2, n_col // 2
     for rnd in range(2):
         a, b = parts[rnd]
         a.gather_end()
-        a.forward()
-        b.pass_on()
+        cut = n_col - n_col // 4 if rnd == 0 else n_col
+        a.forward(0, cut)
+        b.pass_on(1, chips)
+        a.forward(cut, n_col)
         b.gather_end()
-        b.forward()
+        b.forward(0, n_col)
         a.reduce_rows()
+        a.terms(0, 1)
+        if rnd == 1:
+            for part in parts[0]:
+                part.end()
         b.reduce_rows()
-        a.terms(0, n_col)
+        b.terms(0, 1)
+        a.terms(1, n_col)
         a.combine()
-        b.terms(0, n_col // 2)
+        b.terms(1, half)
         a.pair()
-        b.terms(n_col // 2, n_col)
+        b.terms(half, n_col)
         b.combine()
         b.pair()
-        following = parts[1] if rnd == 0 else (None, None)
-        a.reduce_cols(following[0])
-        b.reduce_cols(following[1])
         if rnd == 0:
-            following[0].pass_on()
-
-    for pair in parts:
-        for part in pair:
-            part.end()
+            a.reduce_cols(parts[1][0])
+            parts[1][0].pass_on(1, near)
+            b.reduce_cols(parts[1][1])
+            parts[1][0].pass_on(near, chips)
+        else:
+            a.end()
+            a.reduce_cols(None)
+            b.end()
+            b.reduce_cols(None)
 
 
 def copy_out(*refs):
@@ -301,21 +342,37 @@
         refs[n + j][...] = refs[j][...]
 
 
-def column_order(col, col_count):
-    slots = col.shape[0]
-    ids = jnp.arange(slots, dtype=jnp.int32)
-    key = col * slots + ids
-    rank = jnp.sum((key[None, :] < key[:, None]).astype(jnp.int32), axis=1)
-    hit = (rank[:, None] == ids[None, :]).astype(jnp.int32)
-    perm = jnp.sum(hit * ids[:, None], axis=0)
-    ordered = jnp.sum(hit * col[:, None], axis=0)
-    before = jnp.concatenate([jnp.full((1,), -1, jnp.int32), ordered[:-1]])
-    keep = (ordered == before).astype(F32)
-    js = jnp.arange(col_count, dtype=jnp.int32)
-    upto = jnp.sum((col[None, :] <= js[:, None]).astype(jnp.int32), axis=1)
-    some = jnp.sum((col[None, :] == js[:, None]).astype(jnp.int32), axis=1)
-    last = jnp.where(some > 0, upto - 1, slots)
-    return perm, keep, last
+def column_order(columns, nnz, col_count, perm, keep, last):
+    slots = columns.shape[1]
+    rows = slots // nnz
+    ts = lax.broadcasted_iota(jnp.int32, (rows, slots), 1)
+    block_row = lax.broadcasted_iota(jnp.int32, (rows, slots), 0)
+    parts = [
+        jnp.sum(jnp.where(block_row * nnz + q == ts, columns[...], 0), axis=1, keepdims=True)
+        for q in range(nnz)
+    ]
+    js = lax.broadcasted_iota(jnp.int32, (rows, col_count), 1)
+    ones = jnp.concatenate([(part == js).astype(jnp.int32) for part in parts], axis=0)
+    below = sum(jnp.sum((part < js).astype(jnp.int32), axis=0, keepdims=True) for part in parts)
+    upto = ones
+    step = 1
+    while step < slots:
+        upto = upto + jnp.concatenate([jnp.zeros((step, col_count), jnp.int32), upto[:slots - step]], axis=0)
+        step *= 2
+    held = upto[slots - 1:]
+    last[...] = jnp.where(held > 0, below + held - 1, slots)
+    found, follows = 0, 0
+    for q, part in enumerate(parts):
+        at = slice(q * rows, (q + 1) * rows)
+        before = jnp.sum(ones[at] * (upto[at] - 1), axis=1, keepdims=True)
+        rank = before + jnp.sum(ones[at] * below, axis=1, keepdims=True)
+        rank = jnp.where(part < col_count, rank, slots)
+        slot = block_row * nnz + q
+        hit = rank == ts
+        found += jnp.sum(jnp.where(hit, slot, 0), axis=0, keepdims=True)
+        follows += jnp.sum(jnp.where(hit & (before > 0), 1, 0), axis=0, keepdims=True)
+    perm[...] = found
+    keep[...] = follows.astype(F32)
 
 
 def body(n_row, n_col, blocks, columns, counts, vectors):
@@ -326,32 +383,33 @@
     cols = n_row * vb
     chips = n_row // 2
     active = jnp.arange(nnz, dtype=jnp.int32)[None, :] < counts
-    gcol = jnp.where(active, columns, cols).astype(jnp.int32).reshape(slots)
-    perm, keep, last = column_order(gcol, cols)
+    gcol = jnp.where(active, columns, cols).astype(jnp.int32).reshape(1, slots)
     any_space = pl.BlockSpec(memory_space=pl.ANY)
-    smem = pl.BlockSpec(memory_space=pltpu.SMEM)
     vmem = pl.BlockSpec(memory_space=pltpu.VMEM)
     dma = pltpu.SemaphoreType.DMA
+    order = [((1, slots), jnp.int32), ((1, slots), F32), ((1, cols), jnp.int32)]
     result = [jax.ShapeDtypeStruct((vb, k, bs), BF16)] * 4
     outs = pl.pallas_call(
         functools.partial(kernel, n_row, n_col, vb),
         out_shape=result,
-        in_specs=[any_space, smem, smem, smem, smem, vmem],
+        in_specs=[any_space, vmem, vmem],
         out_specs=[vmem] * 4,
         scratch_shapes=[
+            *[space(shape, kind) for space in (pltpu.VMEM, pltpu.SMEM) for shape, kind in order],
+            pltpu.SMEM((1, slots), jnp.int32),
             pltpu.VMEM((slots, bs, bs), BF16),
             pltpu.VMEM((slots, bs, bs), BF16),
             *[pltpu.VMEM((cols + 1, k2, bs), BF16)] * 4,
             pltpu.VMEM((4, n_col, vb, k2, bs), BF16),
             pltpu.VMEM((4, n_col, vb, k2, bs), BF16),
             pltpu.VMEM((4, rows, k2, bs), BF16),
-            pltpu.VMEM((slots, k2, bs), F32),
-            pltpu.VMEM((slots + 1, k2, bs), F32),
+            *[pltpu.VMEM((slots, k2, bs), F32)] * 2,
+            pltpu.VMEM((slots + 1, k2, bs), BF16),
             pltpu.VMEM((4, n_row, vb, k2, bs), BF16),
             pltpu.VMEM((4, chips, vb, k2, bs), BF16),
             pltpu.VMEM((4, chips, vb, k2, bs), BF16),
             pltpu.VMEM((4, chips, vb, k2, bs), BF16),
-            dma((n_col,)),
+            dma((n_col,)), dma((4,)),
             dma((4, chips)), dma((4, chips)),
             dma((4, chips)), dma((4, chips)),
             dma((4, n_col)), dma((4, n_col)),
@@ -362,7 +420,7 @@
         compiler_params=pltpu.CompilerParams(
             collective_id=0, has_side_effects=True, vmem_limit_bytes=58 << 20),
         name="krylov",
-    )(blocks.reshape(slots, bs, bs), gcol, perm, keep, last, vectors)
+    )(blocks.reshape(slots, bs, bs), gcol, vectors)
     outs = pl.pallas_call(
         copy_out,
         out_shape=result,

time: 92.8 us -> 89.4 us (0.963)
  other arithmetic: 3.09 us -> 0.69 us
  Pallas kernels: 88.7 us -> 87.1 us
    pallas_call x1, Pallas kernels: 87 us -> 85.4 us  [body(): pl.pallas_call(functools.partial(kernel, n_row, n_col, vb), out_shape=res...]
    reduce_sum x3 -> x0, other arithmetic: 1.22 us -> none  [the longest x1 0.84 us: column_order(): ordered = jnp.sum(hit * col[:, None], axis=0)]
where the time goes in v3:
time: 89.4 us; the launch traced here: 89.2 us
  Pallas kernels  87.1 us (97%)
    pallas_call x1, Pallas kernels, body(): pl.pallas_call(functools.partial(kernel, n_row, n_col, vb), out_shape=res...  85.4 us

profile of v3, /device:TPU:1, one launch (start us, length us, event | category | flops | bytes accessed | tf_op | source)
XLA Modules:
  0.0 89.2 jit_solution(844315844360511657)
XLA Ops:
  0.6 0.7 fusion
  1.3 0.1 copy.9
  1.4 0.7 reshape.15.columns
  2.1 85.4 %krylov.1 = (bf16[8,32,128]{2,1,0:T(8,128)(2,1)}, bf16[8,32,128]{2,1,0:T(8,128)(2,1)}, bf16[8,32,128]{2,1,0:T(8,128)(2,1)}, bf16[8,32,128]{2,1,0:T(8,128)(2,1)}) custom-call(bf16[512,128,128]{2,1,0:T(8,128)(2,1)} %bitcast.2, s32[1,512]{1,0:T(1,128)} %reshape.15.columns, bf16[8,32,128]{2,1,0:T(8,128)(2,1)} %vectors.1), custom_call_target="tpu_custom_call" | custom-call | tf_op jit(solution)/shard_map/krylov/pallas_call | solution.py:392
  87.5 1.6 %results.1 = (bf16[8,32,128]{2,1,0:T(8,128)(2,1)}, bf16[8,32,128]{2,1,0:T(8,128)(2,1)}, bf16[8,32,128]{2,1,0:T(8,128)(2,1)}, bf16[8,32,128]{2,1,0:T(8,128)(2,1)}) custom-call(bf16[8,32,128]{2,1,0:T(8,128)(2,1)} %get-tuple-element.8.refs_0_, bf16[8,32,128]{2,1,0:T(8,128)(2,1)} %get-tuple-element.9.refs_1_, bf16[8,32,128]{2,1,0:T(8,128)(2,1)} %get-tuple-element.10.refs_2_, ...), custom_call_target="tpu_custom_call" | custom-call | tf_op jit(solution)/shard_map/results/pallas_call | solution.py:424

commit v4 on v3

--- a/solution.py
+++ b/solution.py
@@ -285,21 +285,17 @@
         lax.fori_loop(0, vb * nnz, one, 0, unroll=8)
         return c
 
-    column_order(columns, nnz, cols, perm_v, keep_v, last_v)
     moves = [
         pltpu.make_async_copy(src, dst, order_sem.at[j])
-        for j, (src, dst) in enumerate(((perm_v, perm), (keep_v, keep), (last_v, last), (columns, gcol)))
+        for j, (src, dst) in enumerate(((columns, gcol), (perm_v, perm), (keep_v, keep), (last_v, last)))
     ]
-    for move in moves:
-        move.start()
-    for move in moves:
-        move.wait()
-
+    moves[0].start()
     early = n_col - n_col // 4
     lax.fori_loop(0, early, turn, 0)
     a.pass_on(1, chips)
     lax.fori_loop(early, n_col, turn, 0)
 
+    moves[0].wait()
     near, half = (chips + 1) // 2, n_col // 2
     for rnd in range(2):
         a, b = parts[rnd]
@@ -312,10 +308,17 @@
         b.forward(0, n_col)
         a.reduce_rows()
         a.terms(0, 1)
-        if rnd == 1:
+        if rnd == 0:
+            column_order(columns, nnz, cols, perm_v, keep_v, last_v)
+            for move in moves[1:]:
+                move.start()
+        else:
             for part in parts[0]:
                 part.end()
         b.reduce_rows()
+        if rnd == 0:
+            for move in moves[1:]:
+                move.wait()
         b.terms(0, 1)
         a.terms(1, n_col)
         a.combine()

time: 89.4 us -> 87.8 us (0.982)
  Pallas kernels: 87.1 us -> 85.5 us
    pallas_call x1, Pallas kernels: 85.4 us -> 83.9 us  [body(): pl.pallas_call(functools.partial(kernel, n_row, n_col, vb), out_shape=res...]
where the time goes in v4:
time: 87.8 us; the launch traced here: 87.6 us
  Pallas kernels  85.5 us (97%)
    pallas_call x1, Pallas kernels, body(): pl.pallas_call(functools.partial(kernel, n_row, n_col, vb), out_shape=res...  83.9 us

profile of v4, /device:TPU:1, one launch (start us, length us, event | category | flops | bytes accessed | tf_op | source)
XLA Modules:
  0.0 87.6 jit_solution(12587255639245988490)
XLA Ops:
  0.6 0.7 fusion
  1.3 0.1 copy.9
  1.4 0.7 reshape.15.columns
  2.1 83.9 %krylov.1 = (bf16[8,32,128]{2,1,0:T(8,128)(2,1)}, bf16[8,32,128]{2,1,0:T(8,128)(2,1)}, bf16[8,32,128]{2,1,0:T(8,128)(2,1)}, bf16[8,32,128]{2,1,0:T(8,128)(2,1)}) custom-call(bf16[512,128,128]{2,1,0:T(8,128)(2,1)} %bitcast.2, s32[1,512]{1,0:T(1,128)} %reshape.15.columns, bf16[8,32,128]{2,1,0:T(8,128)(2,1)} %vectors.1), custom_call_target="tpu_custom_call" | custom-call | tf_op jit(solution)/shard_map/krylov/pallas_call | solution.py:395
  86.0 1.6 %results.1 = (bf16[8,32,128]{2,1,0:T(8,128)(2,1)}, bf16[8,32,128]{2,1,0:T(8,128)(2,1)}, bf16[8,32,128]{2,1,0:T(8,128)(2,1)}, bf16[8,32,128]{2,1,0:T(8,128)(2,1)}) custom-call(bf16[8,32,128]{2,1,0:T(8,128)(2,1)} %get-tuple-element.8.refs_0_, bf16[8,32,128]{2,1,0:T(8,128)(2,1)} %get-tuple-element.9.refs_1_, bf16[8,32,128]{2,1,0:T(8,128)(2,1)} %get-tuple-element.10.refs_2_, ...), custom_call_target="tpu_custom_call" | custom-call | tf_op jit(solution)/shard_map/results/pallas_call | solution.py:427
